TPU v7x, 32 devices: a whole 2x2x4 slice. The times are simulated.
32 devices in a mesh: tm: 4 (over z), rows: 8 (over y, x, core).
Axes of the slice: x: 2, y: 2, z: 4, core: 2. Of those that a mesh axis runs over, the one named last changes fastest.
Arguments:
- features: bfloat16 [4, 128, 64, 256], P('tm', 'rows'), may hold values from -6 to 6
- block_shift: int32 [3, 4, 4, 16, 32], P(None, None, 'tm', 'rows'), may hold values from -5 to 5
- quarter_pel: int32 [3, 4, 4, 16, 32], P(None, None, 'tm', 'rows'), may hold values from 0 to 3
- update_mask: int32 [3, 4], P(None, 'tm'), may hold values 0 or 1
- uniting_weight: bfloat16 [3, 3, 64, 192], replicated, may hold values from -0.15625 to 0.15625
- mixing_weight: bfloat16 [3, 3, 64, 64], replicated, may hold values from -0.25 to 0.25
Outputs:
- refined: bfloat16 [4, 128, 64, 256], P('tm', 'rows')
All inputs are finite; a program needn't handle non-finite values. No bound on the sum of `update_mask` on one device may be relied on, other than what follows from the above.
Results may differ from a plain program's by a relative error of at most 0.0057.
Values may be sent and summed in bfloat16 or wider, within the bound.
A program may use at most 128 MiB of HBM per device.

v0:
```python
import jax
import jax.numpy as jnp
from jax import lax
from jax.sharding import PartitionSpec as P

LEVELS = 3
SPAN = 5


def passed_along(block, axis, distance):
    devices = range(lax.axis_size(axis))
    route = [((i - distance) % len(devices), i) for i in devices]
    return lax.ppermute(block, axis, route)


def with_halo(cells, sides, width):
    for axis, dim in sides:
        count = lax.axis_size(axis)
        ends = count - 1
        head = lax.slice_in_dim(cells, 0, width, axis=dim)
        tail = lax.slice_in_dim(cells, cells.shape[dim] - width, cells.shape[dim], axis=dim)
        cells = jnp.concatenate(
            [
                lax.ppermute(tail, axis, [(i, (i + 1) % count) for i in range(ends)]),
                cells,
                lax.ppermute(head, axis, [((i + 1) % count, i) for i in range(ends)]),
            ],
            axis=dim,
        )
    return cells


def warp_band(extended, shifts, quarters):
    margin = SPAN + 1
    span_rows = extended.shape[0]
    local_rows = span_rows - 2 * margin
    channels = extended.shape[1]
    columns = extended.shape[2]
    wide_cols = columns + 2 * margin
    window_rows = 8 + 2 * margin
    padded = jnp.pad(extended, ((0, 0), (0, 0), (margin, margin)))
    source_cols = jnp.arange(wide_cols, dtype=jnp.int32)[:, None]
    target_cols = jnp.arange(columns, dtype=jnp.int32)[None, :]
    source_rows = jnp.arange(window_rows, dtype=jnp.int32)[None, :, None]
    target_rows = jnp.arange(8, dtype=jnp.int32)[:, None, None]
    outputs = []
    for block_row in range(local_rows // 8):
        shift_rows = jnp.repeat(shifts[0][block_row], 8)
        shift_cols = jnp.repeat(shifts[1][block_row], 8)
        part_rows = jnp.repeat(quarters[0][block_row], 8).astype(jnp.float32) * 0.25
        part_cols = jnp.repeat(quarters[1][block_row], 8).astype(jnp.float32) * 0.25
        col_base = target_cols + shift_cols[None, :] + margin
        col_matrix = (
            jnp.where(source_cols == col_base, 1.0 - part_cols[None, :], 0.0)
            + jnp.where(source_cols == col_base + 1, part_cols[None, :], 0.0)
        ).astype(jnp.bfloat16)
        row_base = target_rows + shift_rows[None, None, :] + margin
        row_tensor = jnp.where(
            source_rows == row_base, 1.0 - part_rows[None, None, :], 0.0
        ) + jnp.where(source_rows == row_base + 1, part_rows[None, None, :], 0.0)
        window = padded[8 * block_row : 8 * block_row + window_rows].reshape(
            window_rows * channels, wide_cols
        )
        column_pass = jnp.dot(window, col_matrix, preferred_element_type=jnp.float32).reshape(
            window_rows, channels, columns
        )
        outputs.append(
            jnp.einsum("iux,ucx->icx", row_tensor, column_pass, precision=lax.Precision.HIGHEST)
        )
    return jnp.concatenate(outputs, axis=0).astype(jnp.bfloat16)


def convolve(pieces, weight):
    count_parts, length, channels, columns = pieces.shape
    outputs = weight.shape[2]
    blocks = weight.reshape(3, 3, outputs, count_parts, channels)
    padded = jnp.pad(pieces, ((0, 0), (0, 0), (0, 0), (1, 1)))
    interior = length - 2
    summed = jnp.zeros((interior, outputs, columns), jnp.float32)
    for tap_row in range(3):
        for tap_col in range(3):
            window = padded[:, tap_row : tap_row + interior, :, tap_col : tap_col + columns]
            summed = summed + jnp.einsum(
                "opc,phcw->how",
                blocks[tap_row, tap_col],
                window,
                preferred_element_type=jnp.float32,
            )
    return summed


def move_earlier_wide(panel_band, ahead_by):
    if ahead_by == 0:
        return panel_band
    return passed_along(panel_band, "tm", ahead_by)


def move_later_wide(panel_band, behind):
    if behind == 0:
        return panel_band
    return passed_along(panel_band, "tm", behind)


def shards(features, block_shift, quarter_pel, update_mask, uniting_weight, mixing_weight):
    current = features[0]
    frames = lax.axis_size("tm")
    margin = SPAN + 1
    local_rows = current.shape[0]
    for level_index in range(LEVELS - 1, -1, -1):
        distance = 2**level_index
        ahead_by = distance % frames
        behind = (frames - ahead_by) % frames
        own_shift = block_shift[level_index, :, 0]
        own_quarter = quarter_pel[level_index, :, 0]
        extended = with_halo(current, (("rows", 0),), SPAN + 1)
        earlier = move_earlier_wide(extended, ahead_by)
        following = move_later_wide(extended, behind)
        warped = jnp.stack(
            [
                warp_band(earlier, own_shift[0:2], own_quarter[0:2]),
                warp_band(following, own_shift[2:4], own_quarter[2:4]),
            ]
        )
        warped_ext = with_halo(warped, (("rows", 1),), 1)
        own_ext = extended[margin - 1 : margin + local_rows + 1]
        pieces = jnp.concatenate([warped_ext, own_ext[None]], axis=0)
        uniting_sum = convolve(pieces, uniting_weight)
        activation = (uniting_sum * jax.nn.sigmoid(uniting_sum)).astype(jnp.bfloat16)
        activation_ext = with_halo(activation, (("rows", 0),), 1)
        mixing_sum = convolve(activation_ext[None], mixing_weight)
        current = (
            current.astype(jnp.float32)
            + update_mask[level_index, 0].astype(jnp.float32) * mixing_sum
        ).astype(jnp.bfloat16)
    return current[None]


def solution(mesh):
    placed = (
        P("tm", "rows", None, None),
        P(None, None, "tm", "rows", None),
        P(None, None, "tm", "rows", None),
        P(None, "tm"),
        P(),
        P(),
    )
    return jax.shard_map(
        shards, mesh=mesh, in_specs=placed, out_specs=P("tm", "rows", None, None), check_vma=False
    )
```

profile of v0, /device:TPU:27, one launch (start us, length us, event | category | flops | bytes accessed | tf_op | source)
XLA Modules:
  0.0 333.2 jit_solution(18146240415956987704)
XLA Ops:
  1.1 3.7 %collective-permute-start = (bf16[6,64,256]{2,1,0:T(8,128)(2,1)S(1)}, bf16[6,64,256]{2,1,0:T(8,128)(2,1)S(1)}, u32[]{:S(2)}, u32[]{:S(2)}) collective-permute-start(bf16[6,64,256]{2,1,0:T(8,128)(2,1)S(1)} %get-tuple-element.21), channel_id=1, source_target_pairs={{0,1},{1,2},{2,3},{3,4},{4,5},{5,6},{6,7},{8,9},{9,10},{10,11},{11... | collective-permute-start | bytes 589832 | tf_op jit(solution)/shard_map/ppermute | solution.py:24
  4.8 1.9 collective-permute-start.1
  6.7 1.5 slice_bitcast_fusion.101
  9.5 1.4 multiply_bitcast_fusion.6
  10.9 1.4 multiply_bitcast_fusion
  40.2 2.4 copy.135
  43.9 2.3 copy.136
  47.4 2.2 copy.134
  50.9 2.3 copy.133
  53.2 5.1 %fusion.146 = bf16[1,8,64,256]{2,1,3,0:T(8,128)(2,1)S(1)} fusion(f32[20,64,256]{1,0,2:T(8,128)} %copy.135, f32[256]{0:T(256)} %copy-done.79, s32[8,256]{0,1:T(8,128)S(1)} %get-tuple-element.112, f32[256]{0:T(256)} %broadcast_subtract_fusion.18, s32[8,256]{0,1:T(8,128)S(1)} %get-tuple-element.111), kind=kOutput, calls=%fused_computation.188 | convolution fusion | flops 31793152 | bytes 1591296 | tf_op jit(solution)/shard_map/iux,ucx->icx/dot_general | solution.py:68
  58.4 3.9 %fusion.147 = bf16[1,8,64,256]{2,1,3,0:T(8,128)(2,1)S(1)} fusion(f32[20,64,256]{1,0,2:T(8,128)S(1)} %copy-done.3, f32[256]{0:T(256)S(1)} %copy-done.81, s32[8,256]{0,1:T(8,128)S(1)} %get-tuple-element.116, f32[256]{0:T(256)S(1)} %copy-done.109, s32[8,256]{0,1:T(8,128)S(1)} %get-tuple-element.115), kind=kOutput, calls=%fused_computation.189 | convolution fusion | flops 31793152 | bytes 1591296 | tf_op jit(solution)/shard_map/iux,ucx->icx/dot_general | solution.py:68
  62.4 3.9 %fusion.145 = bf16[1,8,64,256]{2,1,3,0:T(8,128)(2,1)S(1)} fusion(f32[20,64,256]{1,0,2:T(8,128)S(1)} %copy-done.6, f32[256]{0:T(256)S(1)} %copy-done.83, s32[8,256]{0,1:T(8,128)S(1)} %get-tuple-element.108, f32[256]{0:T(256)S(1)} %copy-done.110, s32[8,256]{0,1:T(8,128)S(1)} %get-tuple-element.107), kind=kOutput, calls=%fused_computation.187 | convolution fusion | flops 31793152 | bytes 1591296 | tf_op jit(solution)/shard_map/iux,ucx->icx/dot_general | solution.py:68
  66.4 3.9 %fusion.144 = bf16[1,8,64,256]{2,1,3,0:T(8,128)(2,1)S(1)} fusion(f32[20,64,256]{1,0,2:T(8,128)S(1)} %copy-done.7, f32[256]{0:T(256)S(1)} %copy-done.85, s32[8,256]{0,1:T(8,128)S(1)} %copy-done.26, f32[256]{0:T(256)S(1)} %copy-done.111, s32[8,256]{0,1:T(8,128)S(1)} %copy-done.25), kind=kOutput, calls=%fused_computation.186 | convolution fusion | flops 31793152 | bytes 1591296 | tf_op jit(solution)/shard_map/iux,ucx->icx/dot_general | solution.py:68
  72.1 4.5 %collective-permute-start.2 = (bf16[2,1,64,256]{2,1,3,0:T(2,128)(2,1)}, bf16[2,1,64,256]{2,1,3,0:T(2,128)(2,1)}, u32[]{:S(2)}, u32[]{:S(2)}) collective-permute-start(bf16[2,1,64,256]{2,1,3,0:T(2,128)(2,1)} %get-tuple-element.9), channel_id=1, source_target_pairs={{0,1},{1,2},{2,3},{3,4},{4,5},{5,6},{6,7},{8,9},{9,10},{10,11},{11... | collective-permute-start | bytes 196616 | tf_op jit(solution)/shard_map/ppermute | solution.py:24
  76.6 1.9 collective-permute-start.3
  79.4 2.7 copy.138
  83.2 2.3 collective-permute-done.3
  86.6 1.5 pad_maximum_fusion
  94.0 2.2 collective-permute-start.4
  96.2 2.1 collective-permute-start.5
  100.0 2.3 collective-permute-done.5
  105.7 2.1 collective-permute-start.6
  107.8 2.2 collective-permute-start.7
  110.6 5.1 %collective-permute-done.7 = bf16[6,64,256]{2,1,0:T(8,128)(2,1)S(1)} collective-permute-done((bf16[6,64,256]{2,1,0:T(8,128)(2,1)S(1)}, bf16[6,64,256]{2,1,0:T(8,128)(2,1)S(1)}, u32[]{:S(2)}, u32[]{:S(2)}) %collective-permute-start.7) | collective-permute-done | bytes 196640 | tf_op jit(solution)/shard_map/ppermute | solution.py:26
  119.0 37.5 %collective-permute-done.8 = bf16[28,64,256]{2,1,0:T(8,128)(2,1)S(1)} collective-permute-done((bf16[28,64,256]{2,1,0:T(8,128)(2,1)S(1)}, bf16[28,64,256]{2,1,0:T(8,128)(2,1)S(1)}, u32[]{:S(2)}, u32[]{:S(2)}) %collective-permute-start.8) | collective-permute-done | bytes 917536 | tf_op jit(solution)/shard_map/ppermute | solution.py:13
  157.2 2.7 copy.154
  160.5 2.3 copy.155
  163.3 2.3 copy.156
  166.3 2.2 copy.157
  168.6 5.1 %fusion.148 = bf16[1,8,64,256]{2,1,3,0:T(8,128)(2,1)S(1)} fusion(f32[20,64,256]{1,0,2:T(8,128)} %copy.154, f32[256]{0:T(256)S(1)} %copy-done.70, s32[8,256]{0,1:T(8,128)S(1)} %copy-done.20, f32[256]{0:T(256)S(1)} %copy-done.104, s32[8,256]{0,1:T(8,128)S(1)} %copy-done.19), kind=kOutput, calls=%fused_computation.190 | convolution fusion | flops 31793152 | bytes 1591296 | tf_op jit(solution)/shard_map/iux,ucx->icx/dot_general | solution.py:68
  173.8 3.9 %fusion.149 = bf16[1,8,64,256]{2,1,3,0:T(8,128)(2,1)S(1)} fusion(f32[20,64,256]{1,0,2:T(8,128)S(1)} %copy-done.2, f32[256]{0:T(256)S(1)} %copy-done.74, s32[8,256]{0,1:T(8,128)S(1)} %copy-done.22, f32[256]{0:T(256)S(1)} %copy-done.105, s32[8,256]{0,1:T(8,128)S(1)} %copy-done.21), kind=kOutput, calls=%fused_computation.191 | convolution fusion | flops 31793152 | bytes 1591296 | tf_op jit(solution)/shard_map/iux,ucx->icx/dot_general | solution.py:68
  177.7 3.9 %fusion.150 = bf16[1,8,64,256]{2,1,3,0:T(8,128)(2,1)S(1)} fusion(f32[20,64,256]{1,0,2:T(8,128)S(1)} %copy-done.4, f32[256]{0:T(256)S(1)} %copy-done.76, s32[8,256]{0,1:T(8,128)S(1)} %get-tuple-element.96, f32[256]{0:T(256)S(1)} %copy-done.106, s32[8,256]{0,1:T(8,128)S(1)} %get-tuple-element.95), kind=kOutput, calls=%fused_computation.192 | convolution fusion | flops 31793152 | bytes 1591296 | tf_op jit(solution)/shard_map/iux,ucx->icx/dot_general | solution.py:68
  181.7 3.9 %fusion.151 = bf16[1,8,64,256]{2,1,3,0:T(8,128)(2,1)S(1)} fusion(f32[20,64,256]{1,0,2:T(8,128)S(1)} %copy-done.8, f32[256]{0:T(256)S(1)} %copy-done.78, s32[8,256]{0,1:T(8,128)S(1)} %get-tuple-element.100, f32[256]{0:T(256)S(1)} %copy-done.107, s32[8,256]{0,1:T(8,128)S(1)} %get-tuple-element.99), kind=kOutput, calls=%fused_computation.193 | convolution fusion | flops 31793152 | bytes 1591296 | tf_op jit(solution)/shard_map/iux,ucx->icx/dot_general | solution.py:68
  187.3 2.1 collective-permute-start.9
  189.4 2.2 collective-permute-start.10
  191.7 2.7 copy.159
  195.5 2.7 collective-permute-done.10
  198.4 1.5 pad_maximum_fusion.1
  205.7 1.9 collective-permute-start.11
  207.7 2.4 collective-permute-start.12
  211.6 2.2 collective-permute-done.12
  217.1 1.9 collective-permute-start.13
  219.1 2.4 collective-permute-start.14
  222.0 4.9 %collective-permute-done.14 = bf16[6,64,256]{2,1,0:T(8,128)(2,1)S(1)} collective-permute-done((bf16[6,64,256]{2,1,0:T(8,128)(2,1)S(1)}, bf16[6,64,256]{2,1,0:T(8,128)(2,1)S(1)}, u32[]{:S(2)}, u32[]{:S(2)}) %collective-permute-start.14) | collective-permute-done | bytes 196640 | tf_op jit(solution)/shard_map/ppermute | solution.py:26
  229.7 1.5 collective-permute-start.16
  232.5 35.6 %collective-permute-done.15 = bf16[28,64,256]{2,1,0:T(8,128)(2,1)S(1)} collective-permute-done((bf16[28,64,256]{2,1,0:T(8,128)(2,1)}, bf16[28,64,256]{2,1,0:T(8,128)(2,1)S(1)}, u32[]{:S(2)}, u32[]{:S(2)}) %collective-permute-start.15) | collective-permute-done | bytes 917536 | tf_op jit(solution)/shard_map/ppermute | solution.py:13
  268.8 2.5 copy.165
  271.9 2.2 copy.166
  274.1 1.7 fusion.54
  275.8 2.3 copy.167
  278.2 1.6 fusion.52
  279.9 2.3 copy.168
  282.2 5.1 %fusion.152 = bf16[1,8,64,256]{2,1,3,0:T(8,128)(2,1)S(1)} fusion(f32[20,64,256]{1,0,2:T(8,128)} %copy.165, f32[256]{0:T(256)S(1)} %copy-done.68, s32[8,256]{0,1:T(8,128)S(1)} %copy-done.24, f32[256]{0:T(256)S(1)} %copy-done.103, s32[8,256]{0,1:T(8,128)S(1)} %copy-done.23), kind=kOutput, calls=%fused_computation.194 | convolution fusion | flops 31793152 | bytes 1591296 | tf_op jit(solution)/shard_map/iux,ucx->icx/dot_general | solution.py:68
  287.4 3.9 %fusion.153 = bf16[1,8,64,256]{2,1,3,0:T(8,128)(2,1)S(1)} fusion(f32[20,64,256]{1,0,2:T(8,128)S(1)} %copy-done.1, f32[256]{0:T(256)S(1)} %copy-done.72, s32[8,256]{0,1:T(8,128)S(1)} %copy-done.29, f32[256]{0:T(256)S(1)} %copy-done.108, s32[8,256]{0,1:T(8,128)S(1)} %copy-done.28), kind=kOutput, calls=%fused_computation.195 | convolution fusion | flops 31793152 | bytes 1591296 | tf_op jit(solution)/shard_map/iux,ucx->icx/dot_general | solution.py:68
  291.4 3.9 %fusion.154 = bf16[1,8,64,256]{2,1,3,0:T(8,128)(2,1)S(1)} fusion(f32[20,64,256]{1,0,2:T(8,128)S(1)} %copy-done.5, f32[256]{0:T(256)S(1)} %copy-done.87, s32[8,256]{0,1:T(8,128)S(1)} %get-tuple-element.80, f32[256]{0:T(256)S(1)} %copy-done.112, s32[8,256]{0,1:T(8,128)S(1)} %get-tuple-element.79), kind=kOutput, calls=%fused_computation.196 | convolution fusion | flops 31793152 | bytes 1591296 | tf_op jit(solution)/shard_map/iux,ucx->icx/dot_general | solution.py:68
  295.4 3.9 %fusion.155 = bf16[1,8,64,256]{2,1,3,0:T(8,128)(2,1)S(1)} fusion(f32[20,64,256]{1,0,2:T(8,128)S(1)} %copy-done.9, f32[256]{0:T(256)S(1)} %copy-done.89, s32[8,256]{0,1:T(8,128)S(1)} %copy-done.27, f32[256]{0:T(256)S(1)} %copy-done.113, s32[8,256]{0,1:T(8,128)S(1)} %get-tuple-element.83), kind=kOutput, calls=%fused_computation.197 | convolution fusion | flops 31793152 | bytes 1591296 | tf_op jit(solution)/shard_map/iux,ucx->icx/dot_general | solution.py:68
  301.0 1.9 collective-permute-start.17
  302.9 2.4 collective-permute-start.18
  305.3 1.9 slice_bitcast_fusion
  307.3 2.7 copy.170
  311.9 1.7 pad_maximum_fusion.2
  319.4 3.4 %collective-permute-start.19 = (bf16[1,64,256]{2,1,0:T(8,128)(2,1)S(1)}, bf16[1,64,256]{2,1,0:T(8,128)(2,1)S(1)}, u32[]{:S(2)}, u32[]{:S(2)}) collective-permute-start(bf16[1,64,256]{2,1,0:T(8,128)(2,1)S(1)} %get-tuple-element.11), channel_id=1, source_target_pairs={{0,1},{1,2},{2,3},{3,4},{4,5},{5,6},{6,7},{8,9},{9,10},{10,11},{11... | collective-permute-start | bytes 98312 | tf_op jit(solution)/shard_map/ppermute | solution.py:24
  322.8 1.9 collective-permute-start.20
  325.4 3.5 %collective-permute-done.20 = bf16[1,64,256]{2,1,0:T(8,128)(2,1)S(1)} collective-permute-done((bf16[1,64,256]{2,1,0:T(8,128)(2,1)S(1)}, bf16[1,64,256]{2,1,0:T(8,128)(2,1)S(1)}, u32[]{:S(2)}, u32[]{:S(2)}) %collective-permute-start.20) | collective-permute-done | bytes 32800 | tf_op jit(solution)/shard_map/ppermute | solution.py:26
  (479 shorter events, 86.4 us)
Async XLA Ops:
  0.0 23.1 %copy-start.18 = (bf16[3,3,64,192]{3,2,1,0:T(8,128)(2,1)S(1)}, bf16[3,3,64,192]{3,2,1,0:T(8,128)(2,1)}, u32[]{:S(2)}) copy-start(bf16[3,3,64,192]{3,2,1,0:T(8,128)(2,1)} %param.10) | copy-start | bytes 663556
  1.1 37.6 %collective-permute-start = (bf16[6,64,256]{2,1,0:T(8,128)(2,1)S(1)}, bf16[6,64,256]{2,1,0:T(8,128)(2,1)S(1)}, u32[]{:S(2)}, u32[]{:S(2)}) collective-permute-start(bf16[6,64,256]{2,1,0:T(8,128)(2,1)S(1)} %get-tuple-element.21), channel_id=1, source_target_pairs={{0,1},{1,2},{2,3},{3,4},{4,5},{5,6},{6,7},{8,9},{9,10},{10,11},{11... | collective-permute-start | bytes 589832 | tf_op jit(solution)/shard_map/ppermute | solution.py:24
  4.8 33.9 %collective-permute-start.1 = (bf16[6,64,256]{2,1,0:T(8,128)(2,1)S(1)}, bf16[6,64,256]{2,1,0:T(8,128)(2,1)S(1)}, u32[]{:S(2)}, u32[]{:S(2)}) collective-permute-start(bf16[6,64,256]{2,1,0:T(8,128)(2,1)S(1)} %get-tuple-element.22), channel_id=1, source_target_pairs={{1,0},{2,1},{3,2},{4,3},{5,4},{6,5},{7,6},{9,8},{10,9},{11,10},{12... | collective-permute-start | bytes 589832 | tf_op jit(solution)/shard_map/ppermute | solution.py:26
  13.2 22.5 %copy-start.36 = (f32[256]{0:T(256)}, f32[256]{0:T(256)S(1)}, u32[]{:S(2)}) copy-start(f32[256]{0:T(256)S(1)} %mul.450) | copy-start | bytes 3076
  13.9 24.8 %copy-start = (bf16[1,16,64,256]{3,2,1,0:T(8,128)(2,1)S(1)}, bf16[1,16,64,256]{3,2,1,0:T(8,128)(2,1)}, u32[]{:S(2)}) copy-start(bf16[1,16,64,256]{3,2,1,0:T(8,128)(2,1)} %param.6) | copy-start | bytes 1572868
  15.7 23.0 %copy-start.38 = (f32[256]{0:T(256)}, f32[256]{0:T(256)S(1)}, u32[]{:S(2)}) copy-start(f32[256]{0:T(256)S(1)} %mul.456) | copy-start | bytes 3076
  18.3 20.5 %copy-start.39 = (f32[256]{0:T(256)}, f32[256]{0:T(256)S(1)}, u32[]{:S(2)}) copy-start(f32[256]{0:T(256)S(1)} %mul.444) | copy-start | bytes 3076
  20.8 17.9 %copy-start.40 = (f32[256]{0:T(256)}, f32[256]{0:T(256)S(1)}, u32[]{:S(2)}) copy-start(f32[256]{0:T(256)S(1)} %mul.438) | copy-start | bytes 3076
  53.2 5.1 %copy-start.109 = (f32[256]{0:T(256)S(1)}, f32[256]{0:T(256)}, u32[]{:S(2)}) copy-start(f32[256]{0:T(256)} %broadcast_subtract_fusion.16) | copy-start | bytes 3076
  72.1 10.0 %collective-permute-start.2 = (bf16[2,1,64,256]{2,1,3,0:T(2,128)(2,1)}, bf16[2,1,64,256]{2,1,3,0:T(2,128)(2,1)}, u32[]{:S(2)}, u32[]{:S(2)}) collective-permute-start(bf16[2,1,64,256]{2,1,3,0:T(2,128)(2,1)} %get-tuple-element.9), channel_id=1, source_target_pairs={{0,1},{1,2},{2,3},{3,4},{4,5},{5,6},{6,7},{8,9},{9,10},{10,11},{11... | collective-permute-start | bytes 196616 | tf_op jit(solution)/shard_map/ppermute | solution.py:24
  76.6 8.9 %collective-permute-start.3 = (bf16[2,1,64,256]{2,1,3,0:T(2,128)(2,1)}, bf16[2,1,64,256]{2,1,3,0:T(2,128)(2,1)}, u32[]{:S(2)}, u32[]{:S(2)}) collective-permute-start(bf16[2,1,64,256]{2,1,3,0:T(2,128)(2,1)} %get-tuple-element.10), channel_id=1, source_target_pairs={{1,0},{2,1},{3,2},{4,3},{5,4},{6,5},{7,6},{9,8},{10,9},{11,10},{12... | collective-permute-start | bytes 196616 | tf_op jit(solution)/shard_map/ppermute | solution.py:26
  79.4 7.2 %copy-start.15 = (bf16[1,18,64,256]{3,2,1,0:T(8,128)(2,1)S(1)}, bf16[1,18,64,256]{3,2,1,0:T(8,128)(2,1)}, u32[]{:S(2)}) copy-start(bf16[1,18,64,256]{3,2,1,0:T(8,128)(2,1)} %slice_bitcast_fusion.2) | copy-start | bytes 1769476
  92.8 5.5 %copy-start.43 = (s32[3,1]{0,1:T(1,128)S(1)}, s32[3,1]{0,1:T(1,128)}, u32[]{:S(2)}) copy-start(s32[3,1]{0,1:T(1,128)} %param.9) | copy-start | bytes 40
  92.8 6.9 %copy-start.102 = (f32[32]{0:T(128)S(1)}, f32[32]{0:T(128)}, u32[]{:S(2)}) copy-start(f32[32]{0:T(128)} %get-tuple-element.46) | copy-start | bytes 388
  92.8 7.0 %copy-start.101 = (f32[32]{0:T(128)S(1)}, f32[32]{0:T(128)}, u32[]{:S(2)}) copy-start(f32[32]{0:T(128)} %get-tuple-element.45) | copy-start | bytes 388
  92.8 9.6 %copy-start.16 = (bf16[3,3,64,64]{3,2,1,0:T(8,128)(2,1)S(1)}, bf16[3,3,64,64]{3,2,1,0:T(8,128)(2,1)}, u32[]{:S(2)}) copy-start(bf16[3,3,64,64]{3,2,1,0:T(8,128)(2,1)} %param.11) | copy-start | bytes 221188
  94.0 6.1 %collective-permute-start.4 = (bf16[1,64,256]{2,1,0:T(8,128)(2,1)S(1)}, bf16[1,64,256]{2,1,0:T(8,128)(2,1)S(1)}, u32[]{:S(2)}, u32[]{:S(2)}) collective-permute-start(bf16[1,64,256]{2,1,0:T(8,128)(2,1)S(1)} %get-tuple-element.19), channel_id=1, source_target_pairs={{0,1},{1,2},{2,3},{3,4},{4,5},{5,6},{6,7},{8,9},{9,10},{10,11},{11... | collective-permute-start | bytes 98312 | tf_op jit(solution)/shard_map/ppermute | solution.py:24
  96.2 6.1 %collective-permute-start.5 = (bf16[1,64,256]{2,1,0:T(8,128)(2,1)S(1)}, bf16[1,64,256]{2,1,0:T(8,128)(2,1)S(1)}, u32[]{:S(2)}, u32[]{:S(2)}) collective-permute-start(bf16[1,64,256]{2,1,0:T(8,128)(2,1)S(1)} %get-tuple-element.20), channel_id=1, source_target_pairs={{1,0},{2,1},{3,2},{4,3},{5,4},{6,5},{7,6},{9,8},{10,9},{11,10},{12... | collective-permute-start | bytes 98312 | tf_op jit(solution)/shard_map/ppermute | solution.py:26
  99.8 10.2 %copy-start.32 = (f32[256]{0:T(256)}, f32[256]{0:T(256)S(1)}, u32[]{:S(2)}) copy-start(f32[256]{0:T(256)S(1)} %mul.498) | copy-start | bytes 3076
  100.0 15.9 %copy-start.71 = (f32[256]{0:T(256)}, f32[256]{0:T(256)S(1)}, u32[]{:S(2)}) copy-start(f32[256]{0:T(256)S(1)} %mul.501) | copy-start | bytes 3076
  105.5 11.0 %copy-start.99 = (s32[32]{0:T(128)S(1)}, s32[32]{0:T(128)}, u32[]{:S(2)}) copy-start(s32[32]{0:T(128)} %get-tuple-element.31) | copy-start | bytes 388
  105.5 11.1 %copy-start.98 = (s32[32]{0:T(128)S(1)}, s32[32]{0:T(128)}, u32[]{:S(2)}) copy-start(s32[32]{0:T(128)} %get-tuple-element.29) | copy-start | bytes 388
  105.6 11.3 %copy-start.97 = (s32[32]{0:T(128)S(1)}, s32[32]{0:T(128)}, u32[]{:S(2)}) copy-start(s32[32]{0:T(128)} %get-tuple-element.23) | copy-start | bytes 388
  105.6 11.5 %copy-start.100 = (f32[32]{0:T(128)S(1)}, f32[32]{0:T(128)}, u32[]{:S(2)}) copy-start(f32[32]{0:T(128)} %get-tuple-element.44) | copy-start | bytes 388
  105.6 11.6 %copy-start.96 = (s32[32]{0:T(128)S(1)}, s32[32]{0:T(128)}, u32[]{:S(2)}) copy-start(s32[32]{0:T(128)} %get-tuple-element.65) | copy-start | bytes 388
  105.6 51.0 %copy-start.50 = (s32[256]{0:T(256)S(1)}, s32[256]{0:T(256)}, u32[]{:S(2)}) copy-start(s32[256]{0:T(256)} %get-tuple-element.89) | copy-start | bytes 3076
  105.6 51.0 %copy-start.51 = (s32[256]{0:T(256)S(1)}, s32[256]{0:T(256)}, u32[]{:S(2)}) copy-start(s32[256]{0:T(256)} %get-tuple-element.90) | copy-start | bytes 3076
  105.6 50.9 %copy-start.61 = (f32[256]{0:T(256)S(1)}, f32[256]{0:T(256)}, u32[]{:S(2)}) copy-start(f32[256]{0:T(256)} %broadcast_subtract_fusion.15) | copy-start | bytes 3076
  105.7 4.9 %collective-permute-start.6 = (bf16[6,64,256]{2,1,0:T(8,128)(2,1)S(1)}, bf16[6,64,256]{2,1,0:T(8,128)(2,1)S(1)}, u32[]{:S(2)}, u32[]{:S(2)}) collective-permute-start(bf16[6,64,256]{2,1,0:T(8,128)(2,1)S(1)} %get-tuple-element.17), channel_id=1, source_target_pairs={{0,1},{1,2},{2,3},{3,4},{4,5},{5,6},{6,7},{8,9},{9,10},{10,11},{11... | collective-permute-start | bytes 589832 | tf_op jit(solution)/shard_map/ppermute | solution.py:24
  107.8 7.9 %collective-permute-start.7 = (bf16[6,64,256]{2,1,0:T(8,128)(2,1)S(1)}, bf16[6,64,256]{2,1,0:T(8,128)(2,1)S(1)}, u32[]{:S(2)}, u32[]{:S(2)}) collective-permute-start(bf16[6,64,256]{2,1,0:T(8,128)(2,1)S(1)} %get-tuple-element.18), channel_id=1, source_target_pairs={{1,0},{2,1},{3,2},{4,3},{5,4},{6,5},{7,6},{9,8},{10,9},{11,10},{12... | collective-permute-start | bytes 589832 | tf_op jit(solution)/shard_map/ppermute | solution.py:26
  115.8 40.8 %copy-start.10 = (bf16[28,64,256]{2,1,0:T(8,128)(2,1)}, bf16[28,64,256]{2,1,0:T(8,128)(2,1)S(1)}, u32[]{:S(2)}) copy-start(bf16[28,64,256]{2,1,0:T(8,128)(2,1)S(1)} %pad_maximum_fusion.4) | copy-start | bytes 2752516
  115.8 40.8 %collective-permute-start.8 = (bf16[28,64,256]{2,1,0:T(8,128)(2,1)S(1)}, bf16[28,64,256]{2,1,0:T(8,128)(2,1)S(1)}, u32[]{:S(2)}, u32[]{:S(2)}) collective-permute-start(bf16[28,64,256]{2,1,0:T(8,128)(2,1)S(1)} %pad_maximum_fusion.4), channel_id=1, source_target_pairs={{16,0},{24,8},{0,16},{8,24},{17,1},{25,9},{1,17},{9,25},{18,2},{26... | collective-permute-start | bytes 2752520 | tf_op jit(solution)/shard_map/ppermute | solution.py:13
  117.2 92.9 %copy-start.34 = (f32[256]{0:T(256)}, f32[256]{0:T(256)S(1)}, u32[]{:S(2)}) copy-start(f32[256]{0:T(256)S(1)} %mul.504) | copy-start | bytes 3076
  168.5 5.1 %copy-start.2 = (f32[20,64,256]{1,0,2:T(8,128)S(1)}, f32[20,64,256]{1,0,2:T(8,128)}, u32[]{:S(2)}) copy-start(f32[20,64,256]{1,0,2:T(8,128)} %copy.155) | copy-start | bytes 3932164
  168.5 5.1 %copy-start.21 = (s32[8,256]{0,1:T(8,128)S(1)}, s32[8,256]{0,1:T(8,128)}, u32[]{:S(2)}) copy-start(s32[8,256]{0,1:T(8,128)} %get-tuple-element.91) | copy-start | bytes 24580
  168.5 5.1 %copy-start.22 = (s32[8,256]{0,1:T(8,128)S(1)}, s32[8,256]{0,1:T(8,128)}, u32[]{:S(2)}) copy-start(s32[8,256]{0,1:T(8,128)} %get-tuple-element.92) | copy-start | bytes 24580
  168.6 5.1 %copy-start.74 = (f32[256]{0:T(256)S(1)}, f32[256]{0:T(256)}, u32[]{:S(2)}) copy-start(f32[256]{0:T(256)} %copy-done.73) | copy-start | bytes 3076
  185.6 6.0 %copy-start.11 = (bf16[28,64,256]{2,1,0:T(8,128)(2,1)S(1)}, bf16[28,64,256]{2,1,0:T(8,128)(2,1)}, u32[]{:S(2)}) copy-start(bf16[28,64,256]{2,1,0:T(8,128)(2,1)} %copy-done.10) | copy-start | bytes 2752516
  187.3 7.1 %collective-permute-start.9 = (bf16[2,1,64,256]{2,1,3,0:T(2,128)(2,1)}, bf16[2,1,64,256]{2,1,3,0:T(2,128)(2,1)}, u32[]{:S(2)}, u32[]{:S(2)}) collective-permute-start(bf16[2,1,64,256]{2,1,3,0:T(2,128)(2,1)} %get-tuple-element.7), channel_id=1, source_target_pairs={{0,1},{1,2},{2,3},{3,4},{4,5},{5,6},{6,7},{8,9},{9,10},{10,11},{11... | collective-permute-start | bytes 196616 | tf_op jit(solution)/shard_map/ppermute | solution.py:24
  189.4 8.8 %collective-permute-start.10 = (bf16[2,1,64,256]{2,1,3,0:T(2,128)(2,1)}, bf16[2,1,64,256]{2,1,3,0:T(2,128)(2,1)S(1)}, u32[]{:S(2)}, u32[]{:S(2)}) collective-permute-start(bf16[2,1,64,256]{2,1,3,0:T(2,128)(2,1)} %get-tuple-element.8), channel_id=1, source_target_pairs={{1,0},{2,1},{3,2},{4,3},{5,4},{6,5},{7,6},{9,8},{10,9},{11,10},{12... | collective-permute-start | bytes 196616 | tf_op jit(solution)/shard_map/ppermute | solution.py:26
  204.5 6.7 %copy-start.94 = (f32[32]{0:T(128)S(1)}, f32[32]{0:T(128)}, u32[]{:S(2)}) copy-start(f32[32]{0:T(128)} %get-tuple-element.43) | copy-start | bytes 388
  204.5 6.9 %copy-start.95 = (f32[32]{0:T(128)S(1)}, f32[32]{0:T(128)}, u32[]{:S(2)}) copy-start(f32[32]{0:T(128)} %get-tuple-element.70) | copy-start | bytes 388
  204.6 9.3 %copy-start.17 = (bf16[3,3,64,64]{3,2,1,0:T(8,128)(2,1)S(1)}, bf16[3,3,64,64]{3,2,1,0:T(8,128)(2,1)}, u32[]{:S(2)}) copy-start(bf16[3,3,64,64]{3,2,1,0:T(8,128)(2,1)} %param.11) | copy-start | bytes 221188
  205.7 5.9 %collective-permute-start.11 = (bf16[1,64,256]{2,1,0:T(8,128)(2,1)S(1)}, bf16[1,64,256]{2,1,0:T(8,128)(2,1)S(1)}, u32[]{:S(2)}, u32[]{:S(2)}) collective-permute-start(bf16[1,64,256]{2,1,0:T(8,128)(2,1)S(1)} %get-tuple-element.15), channel_id=1, source_target_pairs={{0,1},{1,2},{2,3},{3,4},{4,5},{5,6},{6,7},{8,9},{9,10},{10,11},{11... | collective-permute-start | bytes 98312 | tf_op jit(solution)/shard_map/ppermute | solution.py:24
  207.7 6.1 %collective-permute-start.12 = (bf16[1,64,256]{2,1,0:T(8,128)(2,1)S(1)}, bf16[1,64,256]{2,1,0:T(8,128)(2,1)S(1)}, u32[]{:S(2)}, u32[]{:S(2)}) collective-permute-start(bf16[1,64,256]{2,1,0:T(8,128)(2,1)S(1)} %get-tuple-element.16), channel_id=1, source_target_pairs={{1,0},{2,1},{3,2},{4,3},{5,4},{6,5},{7,6},{9,8},{10,9},{11,10},{12... | collective-permute-start | bytes 98312 | tf_op jit(solution)/shard_map/ppermute | solution.py:26
  211.4 10.1 %copy-start.86 = (f32[256]{0:T(256)}, f32[256]{0:T(256)S(1)}, u32[]{:S(2)}) copy-start(f32[256]{0:T(256)S(1)} %mul.507) | copy-start | bytes 3076
  211.6 16.5 %copy-start.41 = (f32[256]{0:T(256)}, f32[256]{0:T(256)S(1)}, u32[]{:S(2)}) copy-start(f32[256]{0:T(256)S(1)} %mul.510) | copy-start | bytes 3076
  217.0 11.1 %copy-start.92 = (s32[32]{0:T(128)S(1)}, s32[32]{0:T(128)}, u32[]{:S(2)}) copy-start(s32[32]{0:T(128)} %get-tuple-element.26) | copy-start | bytes 388
  217.0 11.2 %copy-start.90 = (s32[32]{0:T(128)S(1)}, s32[32]{0:T(128)}, u32[]{:S(2)}) copy-start(s32[32]{0:T(128)} %get-tuple-element.24) | copy-start | bytes 388
  217.0 11.4 %copy-start.91 = (s32[32]{0:T(128)S(1)}, s32[32]{0:T(128)}, u32[]{:S(2)}) copy-start(s32[32]{0:T(128)} %get-tuple-element.61) | copy-start | bytes 388
  217.1 11.5 %copy-start.93 = (f32[32]{0:T(128)S(1)}, f32[32]{0:T(128)}, u32[]{:S(2)}) copy-start(f32[32]{0:T(128)} %get-tuple-element.66) | copy-start | bytes 388
  217.1 51.1 %copy-start.31 = (f32[256]{0:T(256)S(1)}, f32[256]{0:T(256)}, u32[]{:S(2)}) copy-start(f32[256]{0:T(256)} %copy-done.30) | copy-start | bytes 3076
  217.1 51.0 %copy-start.44 = (s32[256]{0:T(256)S(1)}, s32[256]{0:T(256)}, u32[]{:S(2)}) copy-start(s32[256]{0:T(256)} %get-tuple-element.73) | copy-start | bytes 3076
  217.1 51.0 %copy-start.45 = (s32[256]{0:T(256)S(1)}, s32[256]{0:T(256)}, u32[]{:S(2)}) copy-start(s32[256]{0:T(256)} %get-tuple-element.74) | copy-start | bytes 3076
  217.1 51.0 %copy-start.60 = (f32[256]{0:T(256)S(1)}, f32[256]{0:T(256)}, u32[]{:S(2)}) copy-start(f32[256]{0:T(256)} %broadcast_subtract_fusion.7) | copy-start | bytes 3076
  217.1 4.9 %collective-permute-start.13 = (bf16[6,64,256]{2,1,0:T(8,128)(2,1)S(1)}, bf16[6,64,256]{2,1,0:T(8,128)(2,1)S(1)}, u32[]{:S(2)}, u32[]{:S(2)}) collective-permute-start(bf16[6,64,256]{2,1,0:T(8,128)(2,1)S(1)} %get-tuple-element.13), channel_id=1, source_target_pairs={{0,1},{1,2},{2,3},{3,4},{4,5},{5,6},{6,7},{8,9},{9,10},{10,11},{11... | collective-permute-start | bytes 589832 | tf_op jit(solution)/shard_map/ppermute | solution.py:24
  219.1 7.9 %collective-permute-start.14 = (bf16[6,64,256]{2,1,0:T(8,128)(2,1)S(1)}, bf16[6,64,256]{2,1,0:T(8,128)(2,1)S(1)}, u32[]{:S(2)}, u32[]{:S(2)}) collective-permute-start(bf16[6,64,256]{2,1,0:T(8,128)(2,1)S(1)} %get-tuple-element.14), channel_id=1, source_target_pairs={{1,0},{2,1},{3,2},{4,3},{5,4},{6,5},{7,6},{9,8},{10,9},{11,10},{12... | collective-permute-start | bytes 589832 | tf_op jit(solution)/shard_map/ppermute | solution.py:26
  228.0 40.1 %collective-permute-start.15 = (bf16[28,64,256]{2,1,0:T(8,128)(2,1)}, bf16[28,64,256]{2,1,0:T(8,128)(2,1)S(1)}, u32[]{:S(2)}, u32[]{:S(2)}) collective-permute-start(bf16[28,64,256]{2,1,0:T(8,128)(2,1)} %pad_maximum_fusion.5), channel_id=1, source_target_pairs={{24,0},{0,8},{8,16},{16,24},{25,1},{1,9},{9,17},{17,25},{26,2},{2,... | collective-permute-start | bytes 2752520 | tf_op jit(solution)/shard_map/ppermute | solution.py:13
  228.8 42.5 %copy-start.88 = (f32[256]{0:T(256)}, f32[256]{0:T(256)S(1)}, u32[]{:S(2)}) copy-start(f32[256]{0:T(256)S(1)} %mul.513) | copy-start | bytes 3076
  229.7 44.4 %collective-permute-start.16 = (bf16[28,64,256]{2,1,0:T(8,128)(2,1)}, bf16[28,64,256]{2,1,0:T(8,128)(2,1)}, u32[]{:S(2)}, u32[]{:S(2)}) collective-permute-start(bf16[28,64,256]{2,1,0:T(8,128)(2,1)} %pad_maximum_fusion.5), channel_id=1, source_target_pairs={{8,0},{16,8},{24,16},{0,24},{9,1},{17,9},{25,17},{1,25},{10,2},{18... | collective-permute-start | bytes 2752520 | tf_op jit(solution)/shard_map/ppermute | solution.py:13
  301.0 9.0 %collective-permute-start.17 = (bf16[2,1,64,256]{2,1,3,0:T(2,128)(2,1)}, bf16[2,1,64,256]{2,1,3,0:T(2,128)(2,1)}, u32[]{:S(2)}, u32[]{:S(2)}) collective-permute-start(bf16[2,1,64,256]{2,1,3,0:T(2,128)(2,1)} %get-tuple-element.5), channel_id=1, source_target_pairs={{0,1},{1,2},{2,3},{3,4},{4,5},{5,6},{6,7},{8,9},{9,10},{10,11},{11... | collective-permute-start | bytes 196616 | tf_op jit(solution)/shard_map/ppermute | solution.py:24
  302.9 8.8 %collective-permute-start.18 = (bf16[2,1,64,256]{2,1,3,0:T(2,128)(2,1)}, bf16[2,1,64,256]{2,1,3,0:T(2,128)(2,1)S(1)}, u32[]{:S(2)}, u32[]{:S(2)}) collective-permute-start(bf16[2,1,64,256]{2,1,3,0:T(2,128)(2,1)} %get-tuple-element.6), channel_id=1, source_target_pairs={{1,0},{2,1},{3,2},{4,3},{5,4},{6,5},{7,6},{9,8},{10,9},{11,10},{12... | collective-permute-start | bytes 196616 | tf_op jit(solution)/shard_map/ppermute | solution.py:26
  319.4 6.1 %collective-permute-start.19 = (bf16[1,64,256]{2,1,0:T(8,128)(2,1)S(1)}, bf16[1,64,256]{2,1,0:T(8,128)(2,1)S(1)}, u32[]{:S(2)}, u32[]{:S(2)}) collective-permute-start(bf16[1,64,256]{2,1,0:T(8,128)(2,1)S(1)} %get-tuple-element.11), channel_id=1, source_target_pairs={{0,1},{1,2},{2,3},{3,4},{4,5},{5,6},{6,7},{8,9},{9,10},{10,11},{11... | collective-permute-start | bytes 98312 | tf_op jit(solution)/shard_map/ppermute | solution.py:24
  322.8 6.1 %collective-permute-start.20 = (bf16[1,64,256]{2,1,0:T(8,128)(2,1)S(1)}, bf16[1,64,256]{2,1,0:T(8,128)(2,1)S(1)}, u32[]{:S(2)}, u32[]{:S(2)}) collective-permute-start(bf16[1,64,256]{2,1,0:T(8,128)(2,1)S(1)} %get-tuple-element.12), channel_id=1, source_target_pairs={{1,0},{2,1},{3,2},{4,3},{5,4},{6,5},{7,6},{9,8},{10,9},{11,10},{12... | collective-permute-start | bytes 98312 | tf_op jit(solution)/shard_map/ppermute | solution.py:26
  (71 other events, 208.0 us)
where the time goes:
time: 337 us; the launch traced here: 333 us
  waiting for transfers between devices  96.8 us (29%)
  matrix products  89.7 us (27%)
  local copies, waits for them, and re-layouts  60.8 us (18%)
  starting transfers between devices  45 us (13%)
  other arithmetic  36.2 us (11%)
  between operations  4.71 us (1%)
    ppermute x3, waiting for transfers between devices, passed_along(): return lax.ppermute(block, axis, route)  73.1 us
    dot_general x12, matrix products, warp_band(): jnp.einsum('iux,ucx->icx', row_tensor, column_pass, precision=lax.Precisi...  50.7 us
    dot_general x12, local copies, waits for them, and re-layouts, warp_band(): jnp.dot(window, col_matrix, preferred_element_type=jnp.float32)  28 us
    dot_general x54, matrix products, convolve(): jnp.einsum('opc,phcw->how', blocks[tap_row, tap_col], window, preferred_e...  27.3 us
    ppermute x9, starting transfers between devices, with_halo(): lax.ppermute(tail, axis, [(i, (i + 1) % count) for i in range(ends)])  23.8 us
    ppermute x9, waiting for transfers between devices, with_halo(): lax.ppermute(head, axis, [((i + 1) % count, i) for i in range(ends)])  23.7 us
    ppermute x9, starting transfers between devices, with_halo(): lax.ppermute(head, axis, [((i + 1) % count, i) for i in range(ends)])  19.6 us
    dot_general x12, matrix products, warp_band(): jnp.dot(window, col_matrix, preferred_element_type=jnp.float32)  11.7 us
  transfers between devices with their start and end apart: 21, of which 10 were waited for; matrix products, arithmetic and copies ran while one was open for 18% of the time, Pallas kernels for 0%

commit v1 on v0

v1 whole, which is shorter than its diff:
```python
import functools

import jax
import jax.numpy as jnp
from jax import lax
from jax.experimental import pallas as pl
from jax.experimental.pallas import tpu as pltpu
from jax.sharding import PartitionSpec as P

LEVELS = 3
SPAN = 5
HALO = 8
REACH = 2
MESH = pl.DeviceIdType.MESH


def plan(frames):
    routes = {}
    for level in range(LEVELS):
        ahead = 2**level % frames
        behind = (frames - ahead) % frames
        if ahead == 0:
            routes[level] = ()
        elif ahead == behind:
            routes[level] = (ahead,)
        else:
            routes[level] = (ahead, behind)
    return routes


def kernel(frames, bands, features, grid_values, mask, uniting, mixing, out, *scratch):
    routes = plan(frames)
    total_refs = sum(len(routes[level]) for level in range(LEVELS))
    own = scratch[0]
    others = scratch[1]
    near, expanded, column_pass, joined, activation, w_unite, w_mix = scratch[2:9]
    send_own, recv_own, send_ref, recv_ref, send_near, recv_near = scratch[9:]
    local = features.shape[0]
    channels, columns = features.shape[1:]
    half = local // 2
    first = {}
    for level in range(LEVELS - 1, -1, -1):
        first[level] = sum(len(routes[k]) for k in range(level + 1, LEVELS))

    t = lax.axis_index("tm")
    r = lax.axis_index("rows")
    has_above = r > 0
    has_below = r < bands - 1
    up = (t, r - 1)
    down = (t, r + 1)
    hops = sorted({h for level in range(LEVELS) for h in routes[level]} | {frames - h for level in range(LEVELS) for h in routes[level]})

    barrier = pltpu.get_barrier_semaphore()

    @pl.when(has_above)
    def _():
        pl.semaphore_signal(barrier, inc=1, device_id=up, device_id_type=MESH)

    @pl.when(has_below)
    def _():
        pl.semaphore_signal(barrier, inc=1, device_id=down, device_id_type=MESH)

    for hop in hops:
        pl.semaphore_signal(barrier, inc=1, device_id=(lax.rem(t + hop, frames), r), device_id_type=MESH)

    zero_rows = jnp.zeros((HALO, channels, columns), jnp.bfloat16)

    @pl.when(jnp.logical_not(has_above))
    def _():
        for k in range(LEVELS):
            own[k, 0:HALO] = zero_rows
        for k in range(total_refs):
            others[k, 0:HALO] = zero_rows
        near[0] = jnp.zeros(near.shape[1:], near.dtype)

    @pl.when(jnp.logical_not(has_below))
    def _():
        for k in range(LEVELS):
            own[k, HALO + local : 2 * HALO + local] = zero_rows
        for k in range(total_refs):
            others[k, HALO + local : 2 * HALO + local] = zero_rows
        near[1] = jnp.zeros(near.shape[1:], near.dtype)

    own[LEVELS - 1, HALO : HALO + local] = features[...]

    pl.semaphore_wait(barrier, len(hops) + jnp.minimum(r, 1) + jnp.minimum(bands - 1 - r, 1))

    def remote(src, dst, send, recv, where):
        return pltpu.make_async_remote_copy(
            src_ref=src, dst_ref=dst, send_sem=send, recv_sem=recv, device_id=where, device_id_type=MESH
        )

    def near_copy(side):
        return remote(grid_values, near.at[side], send_near.at[side], recv_near.at[side], down if side == 0 else up)

    def own_copy(level, side):
        rows = REACH if routes[level] else HALO
        if side == 0:
            src, dst = HALO + local - rows, HALO - rows
        else:
            src, dst = HALO, HALO + local
        return remote(
            own.at[level, pl.ds(src, rows)],
            own.at[level, pl.ds(dst, rows)],
            send_own.at[level, side],
            recv_own.at[level, side],
            down if side == 0 else up,
        )

    def ref_copy(level, which, part):
        slot = first[level] + which
        rows = pl.ds(HALO + part * half, half)
        return remote(
            own.at[level, rows],
            others.at[slot, rows],
            send_ref.at[slot, part],
            recv_ref.at[slot, part],
            (lax.rem(t + routes[level][which], frames), r),
        )

    def edge_copy(level, which, side):
        slot = first[level] + which
        src, dst = (local, 0) if side == 0 else (HALO, HALO + local)
        return remote(
            others.at[slot, pl.ds(src, HALO)],
            others.at[slot, pl.ds(dst, HALO)],
            send_ref.at[slot, 2 + side],
            recv_ref.at[slot, 2 + side],
            down if side == 0 else up,
        )

    def when_sends(side):
        return has_below if side == 0 else has_above

    def when_gets(side):
        return has_above if side == 0 else has_below

    def start(copy, side):
        @pl.when(when_sends(side))
        def _():
            copy.start()

    def received(copy, side):
        @pl.when(when_gets(side))
        def _():
            copy.wait_recv()

    def sent(copy, side):
        @pl.when(when_sends(side))
        def _():
            copy.wait_send()

    def send_part(level, part):
        for which in range(len(routes[level])):
            ref_copy(level, which, part).start()
        start(own_copy(level, 1 - part), 1 - part)

    send_part(LEVELS - 1, 0)
    send_part(LEVELS - 1, 1)
    for side in (0, 1):
        start(near_copy(side), side)

    for tap in range(3):
        w_unite[:, tap * 3 * channels : (tap + 1) * 3 * channels] = uniting[tap].reshape(3 * channels, 3 * channels)
        w_mix[:, tap * channels : (tap + 1) * channels] = mixing[tap].reshape(3 * channels, channels)

    for side in (0, 1):
        received(near_copy(side), side)
    blocks = grid_values.shape[1]
    spread = (
        lax.broadcasted_iota(jnp.int32, (blocks, columns), 1) // 8
        == lax.broadcasted_iota(jnp.int32, (blocks, columns), 0)
    ).astype(jnp.bfloat16)
    for place, values in enumerate((near[0], grid_values[...], near[1])):
        expanded[place] = jnp.dot(values.astype(jnp.bfloat16), spread, preferred_element_type=jnp.float32)

    exists = (jnp.where(has_above, 1.0, 0.0), 1.0, 1.0, jnp.where(has_below, 1.0, 0.0))
    groups = ((-REACH, REACH, 0, 1), (0, 8, 1, 0), (8, 8, 1, 1), (local, REACH, 2, 0))
    quarters_at = grid_values.shape[0] // 2
    source_cols = lax.broadcasted_iota(jnp.int32, (columns, columns), 0).astype(jnp.float32)
    target_cols = lax.broadcasted_iota(jnp.int32, (1, columns), 1).astype(jnp.float32)

    def warp(level, component, source, to_channel):
        for group, (begin, rows, place, block_row) in enumerate(groups):
            y_at = (level * 4 + component) * 2 + block_row
            x_at = y_at + 2
            col_shift = expanded[place, x_at : x_at + 1, :]
            col_part = expanded[place, quarters_at + x_at : quarters_at + x_at + 1, :]
            col_pos = target_cols + col_shift + 0.25 * col_part
            hat = jnp.maximum(1.0 - jnp.abs(source_cols - col_pos), 0.0).astype(jnp.bfloat16)
            window = rows + 2 * SPAN + 1
            seen = source[pl.ds(HALO + begin - SPAN, window)].reshape(window * channels, columns)
            column_pass[0:window] = jnp.dot(seen, hat, preferred_element_type=jnp.float32).reshape(
                window, channels, columns
            )

            def piece(step, carry):
                lanes = pl.ds(pl.multiple_of((step // 4) * 128, 128), 128)
                chans = pl.ds(pl.multiple_of((step % 4) * 16, 16), 16)
                shift = jnp.broadcast_to(expanded[place, y_at : y_at + 1, lanes] + float(SPAN), (16, 128))
                part = jnp.broadcast_to(
                    0.25 * expanded[place, quarters_at + y_at : quarters_at + y_at + 1, lanes], (16, 128)
                )
                lines = [column_pass[i, chans, lanes] for i in range(window)]
                for size in (8, 4, 2, 1):
                    far = shift >= float(size)
                    shift = jnp.where(far, shift - float(size), shift)
                    keep = rows + size
                    lines = [
                        jnp.where(far, lines[i + size], lines[i]) if i + size < len(lines) else lines[i]
                        for i in range(keep)
                    ]
                for i in range(rows):
                    value = lines[i] + part * (lines[i + 1] - lines[i])
                    if group in (0, 3):
                        value = value * exists[group]
                    to = pl.ds(pl.multiple_of(to_channel + (step % 4) * 16, 16), 16)
                    joined[begin + REACH + i, to, lanes] = value.astype(jnp.bfloat16)
                return carry

            lax.fori_loop(0, (channels // 16) * (columns // 128), piece, 0)

    lane = lax.broadcasted_iota(jnp.int32, (channels, columns), 1)
    not_first = lane > 0
    not_last = lane < columns - 1

    def taps(product):
        left, middle, right = (product[i * channels : (i + 1) * channels] for i in range(3))
        return (
            middle
            + jnp.where(not_first, pltpu.roll(left, 1, 1), 0.0)
            + jnp.where(not_last, pltpu.roll(right, columns - 1, 1), 0.0)
        )

    def unite(begin, end):
        def row(y, carry):
            slab = joined[pl.ds(y, 3)].reshape(9 * channels, columns)
            total = taps(jnp.dot(w_unite[...], slab, preferred_element_type=jnp.float32))
            activation[y] = (total * jax.nn.sigmoid(total)).astype(jnp.bfloat16)
            return carry

        lax.fori_loop(begin, end, row, 0)

    def mix(level, begin, end):
        kept = mask[level, 0].astype(jnp.float32)

        def row(y, carry):
            slab = activation[pl.ds(y, 3)].reshape(3 * channels, columns)
            total = taps(jnp.dot(w_mix[...], slab, preferred_element_type=jnp.float32))
            fresh = (own[level, HALO + y].astype(jnp.float32) + kept * total).astype(jnp.bfloat16)
            if level > 0:
                own[level - 1, HALO + y] = fresh
            else:
                out[y] = fresh
            return carry

        lax.fori_loop(begin, end, row, 0)

    for level in range(LEVELS - 1, -1, -1):
        count = len(routes[level])
        for side in (1, 0):
            received(own_copy(level, side), side)
        joined[:, 2 * channels : 3 * channels, :] = own[level, pl.ds(HALO - REACH, local + 2 * REACH)]
        for part in (0, 1):
            for which in range(count):
                ref_copy(level, which, part).wait_recv()
                start(edge_copy(level, which, 1 - part), 1 - part)
        for which in range(2):
            if which < count:
                for side in (1, 0):
                    received(edge_copy(level, which, side), side)
            source = others.at[first[level] + min(which, count - 1)] if count else own.at[level]
            warp(level, 2 * which, source, which * channels)
        unite(0, half + 2)

        @pl.when(jnp.logical_not(has_above))
        def _():
            activation[0] = jnp.zeros((channels, columns), jnp.bfloat16)

        mix(level, 0, half)
        if level > 0:
            send_part(level - 1, 0)
        unite(half + 2, local + 2)

        @pl.when(jnp.logical_not(has_below))
        def _():
            activation[local + 1] = jnp.zeros((channels, columns), jnp.bfloat16)

        mix(level, half, local)
        if level > 0:
            send_part(level - 1, 1)

    for side in (0, 1):
        sent(near_copy(side), side)
        for level in range(LEVELS):
            sent(own_copy(level, side), side)
            for which in range(len(routes[level])):
                ref_copy(level, which, side).wait_send()
                sent(edge_copy(level, which, side), side)


def shards(frames, bands, features, block_shift, quarter_pel, update_mask, uniting_weight, mixing_weight):
    band = features[0]
    local, channels, columns = band.shape
    blocks = block_shift.shape[-1]
    grid_values = jnp.concatenate(
        [block_shift.reshape(-1, blocks), quarter_pel.reshape(-1, blocks)], axis=0
    ).astype(jnp.float32)
    total_refs = max(1, sum(len(route) for route in plan(frames).values()))
    vmem = pl.BlockSpec(memory_space=pltpu.VMEM)
    dma = pltpu.SemaphoreType.DMA
    refined = pl.pallas_call(
        functools.partial(kernel, frames, bands),
        out_shape=jax.ShapeDtypeStruct(band.shape, jnp.bfloat16),
        in_specs=[vmem, vmem, pl.BlockSpec(memory_space=pltpu.SMEM), vmem, vmem],
        out_specs=vmem,
        scratch_shapes=[
            pltpu.VMEM((LEVELS, local + 2 * HALO, channels, columns), jnp.bfloat16),
            pltpu.VMEM((total_refs, local + 2 * HALO, channels, columns), jnp.bfloat16),
            pltpu.VMEM((2,) + grid_values.shape, jnp.float32),
            pltpu.VMEM((3, grid_values.shape[0], columns), jnp.float32),
            pltpu.VMEM((8 + 2 * SPAN + 1, channels, columns), jnp.float32),
            pltpu.VMEM((local + 2 * REACH, 3 * channels, columns), jnp.bfloat16),
            pltpu.VMEM((local + 2, channels, columns), jnp.bfloat16),
            pltpu.VMEM((3 * channels, 9 * channels), jnp.bfloat16),
            pltpu.VMEM((3 * channels, 3 * channels), jnp.bfloat16),
            dma((LEVELS, 2)),
            dma((LEVELS, 2)),
            dma((total_refs, 4)),
            dma((total_refs, 4)),
            dma((2,)),
            dma((2,)),
        ],
        compiler_params=pltpu.CompilerParams(
            collective_id=0, has_side_effects=True, vmem_limit_bytes=40 * 1024 * 1024
        ),
    )(band, grid_values, update_mask, uniting_weight, mixing_weight)
    return refined[None]


def solution(mesh):
    placed = (
        P("tm", "rows", None, None),
        P(None, None, "tm", "rows", None),
        P(None, None, "tm", "rows", None),
        P(None, "tm"),
        P(),
        P(),
    )
    return jax.shard_map(
        functools.partial(shards, mesh.shape["tm"], mesh.shape["rows"]),
        mesh=mesh,
        in_specs=placed,
        out_specs=P("tm", "rows", None, None),
        check_vma=False,
    )
```

time: 337 us -> 103 us (0.31)
  the two profiles are of different devices: /device:TPU:27 before, /device:TPU:4 now
where the time goes in v1:
time: 103 us
  Pallas kernels  98 us (95%)
  local copies, waits for them, and re-layouts  4.45 us (4%)
    pallas_call x1, Pallas kernels, shards(): pl.pallas_call(functools.partial(kernel, frames, bands), out_shape=jax.Sh...  98 us
    unnamed x10, local copies, waits for them, and re-layouts  4.45 us

profile of v1, /device:TPU:4, one launch (start us, length us, event | category | flops | bytes accessed | tf_op | source)
XLA Modules:
  0.0 103.2 jit_solution(5766791654371994698)
XLA Ops:
  0.0 0.0 copy-start.3
  0.0 0.7 copy-done.3
  0.7 0.1 copy.7.mask
  0.7 0.7 add_convert_fusion.grid_values
  1.5 0.0 copy-start
  1.5 1.0 %copy-done = bf16[1,16,64,256]{3,2,1,0:T(8,128)(2,1)S(1)} copy-done((bf16[1,16,64,256]{3,2,1,0:T(8,128)(2,1)S(1)}, bf16[1,16,64,256]{3,2,1,0:T(8,128)(2,1)}, u32[]{:S(2)}) %copy-start) | copy-done | bytes 524312
  2.5 0.0 copy-start.1
  2.5 1.0 copy-done.1
  3.5 0.0 copy-start.2
  3.5 0.9 copy-done.2
  4.4 98.0 %shard_map.64 = bf16[16,64,256]{2,1,0:T(8,128)(2,1)S(1)} custom-call(bf16[16,64,256]{2,1,0:T(8,128)(2,1)S(1)} %bitcast.5, f32[48,32]{1,0:T(8,128)S(1)} %add_convert_fusion.grid_values, s32[3,1]{1,0:T(4,128)S(1)} %copy.7.mask, bf16[3,3,64,192]{3,2,1,0:T(8,128)(2,1)S(1)} %copy-done.1, bf16[3,3,64,64]{3,2,1,0:T(8,128)(2,1)S(1)} %copy-done.2), custom_call_target="tpu_custom_call" | custom-call | tf_op jit(solution)/shard_map/pallas_call | solution.py:312
  102.4 0.8 copy.9
Async XLA Ops:
  0.0 0.7 copy-start.3
  1.5 1.0 %copy-start = (bf16[1,16,64,256]{3,2,1,0:T(8,128)(2,1)S(1)}, bf16[1,16,64,256]{3,2,1,0:T(8,128)(2,1)}, u32[]{:S(2)}) copy-start(bf16[1,16,64,256]{3,2,1,0:T(8,128)(2,1)} %param.6) | copy-start | bytes 1572868
  2.5 1.0 copy-start.1
  3.5 0.9 copy-start.2

commit v2 on v1

--- a/solution.py
+++ b/solution.py
@@ -33,8 +33,8 @@
     total_refs = sum(len(routes[level]) for level in range(LEVELS))
     own = scratch[0]
     others = scratch[1]
-    near, expanded, column_pass, joined, activation, w_unite, w_mix = scratch[2:9]
-    send_own, recv_own, send_ref, recv_ref, send_near, recv_near = scratch[9:]
+    near, expanded, column_pass, joined, activation, w_unite, w_mix, uniting_here, mixing_here, fetched = scratch[2:12]
+    send_own, recv_own, send_ref, recv_ref, send_near, recv_near = scratch[12:]
     local = features.shape[0]
     channels, columns = features.shape[1:]
     half = local // 2
@@ -50,6 +50,15 @@
     down = (t, r + 1)
     hops = sorted({h for level in range(LEVELS) for h in routes[level]} | {frames - h for level in range(LEVELS) for h in routes[level]})
 
+    band_copy = pltpu.make_async_copy(features, own.at[LEVELS - 1, pl.ds(HALO, local)], fetched.at[0])
+    weight_copies = (
+        pltpu.make_async_copy(uniting, uniting_here, fetched.at[1]),
+        pltpu.make_async_copy(mixing, mixing_here, fetched.at[2]),
+    )
+    band_copy.start()
+    for copy in weight_copies:
+        copy.start()
+
     barrier = pltpu.get_barrier_semaphore()
 
     @pl.when(has_above)
@@ -81,7 +90,6 @@
             others[k, HALO + local : 2 * HALO + local] = zero_rows
         near[1] = jnp.zeros(near.shape[1:], near.dtype)
 
-    own[LEVELS - 1, HALO : HALO + local] = features[...]
 
     pl.semaphore_wait(barrier, len(hops) + jnp.minimum(r, 1) + jnp.minimum(bands - 1 - r, 1))
 
@@ -155,14 +163,24 @@
             ref_copy(level, which, part).start()
         start(own_copy(level, 1 - part), 1 - part)
 
+    band_copy.wait()
     send_part(LEVELS - 1, 0)
     send_part(LEVELS - 1, 1)
     for side in (0, 1):
         start(near_copy(side), side)
 
-    for tap in range(3):
-        w_unite[:, tap * 3 * channels : (tap + 1) * 3 * channels] = uniting[tap].reshape(3 * channels, 3 * channels)
-        w_mix[:, tap * channels : (tap + 1) * channels] = mixing[tap].reshape(3 * channels, channels)
+    tall = 3 * channels
+    w_unite[...] = jnp.zeros_like(w_unite)
+    w_mix[...] = jnp.zeros_like(w_mix)
+    for copy in weight_copies:
+        copy.wait()
+    for pair in range(2):
+        for tap in range(3):
+            at = pair + tap
+            w_unite[pair * tall : (pair + 1) * tall, at * tall : (at + 1) * tall] = uniting_here[tap].reshape(tall, tall)
+            w_mix[pair * tall : (pair + 1) * tall, at * channels : (at + 1) * channels] = mixing_here[tap].reshape(
+                tall, channels
+            )
 
     for side in (0, 1):
         received(near_copy(side), side)
@@ -218,7 +236,7 @@
                     joined[begin + REACH + i, to, lanes] = value.astype(jnp.bfloat16)
                 return carry
 
-            lax.fori_loop(0, (channels // 16) * (columns // 128), piece, 0)
+            lax.fori_loop(0, (channels // 16) * (columns // 128), piece, 0, unroll=4)
 
     lane = lax.broadcasted_iota(jnp.int32, (channels, columns), 1)
     not_first = lane > 0
@@ -233,28 +251,34 @@
         )
 
     def unite(begin, end):
-        def row(y, carry):
-            slab = joined[pl.ds(y, 3)].reshape(9 * channels, columns)
-            total = taps(jnp.dot(w_unite[...], slab, preferred_element_type=jnp.float32))
-            activation[y] = (total * jax.nn.sigmoid(total)).astype(jnp.bfloat16)
+        def rows(step, carry):
+            y = begin + 2 * step
+            slab = joined[pl.ds(y, 4)].reshape(12 * channels, columns)
+            product = jnp.dot(w_unite[...], slab, preferred_element_type=jnp.float32)
+            for pair in range(2):
+                total = taps(product[pair * tall : (pair + 1) * tall])
+                activation[y + pair] = (total * jax.nn.sigmoid(total)).astype(jnp.bfloat16)
             return carry
 
-        lax.fori_loop(begin, end, row, 0)
+        lax.fori_loop(0, (end - begin) // 2, rows, 0, unroll=True)
 
     def mix(level, begin, end):
         kept = mask[level, 0].astype(jnp.float32)
 
-        def row(y, carry):
-            slab = activation[pl.ds(y, 3)].reshape(3 * channels, columns)
-            total = taps(jnp.dot(w_mix[...], slab, preferred_element_type=jnp.float32))
-            fresh = (own[level, HALO + y].astype(jnp.float32) + kept * total).astype(jnp.bfloat16)
-            if level > 0:
-                own[level - 1, HALO + y] = fresh
-            else:
-                out[y] = fresh
+        def rows(step, carry):
+            y = begin + 2 * step
+            slab = activation[pl.ds(y, 4)].reshape(4 * channels, columns)
+            product = jnp.dot(w_mix[...], slab, preferred_element_type=jnp.float32)
+            for pair in range(2):
+                total = taps(product[pair * tall : (pair + 1) * tall])
+                fresh = (own[level, HALO + y + pair].astype(jnp.float32) + kept * total).astype(jnp.bfloat16)
+                if level > 0:
+                    own[level - 1, HALO + y + pair] = fresh
+                else:
+                    out[y + pair] = fresh
             return carry
 
-        lax.fori_loop(begin, end, row, 0)
+        lax.fori_loop(0, (end - begin) // 2, rows, 0, unroll=True)
 
     for level in range(LEVELS - 1, -1, -1):
         count = len(routes[level])
@@ -308,11 +332,12 @@
     ).astype(jnp.float32)
     total_refs = max(1, sum(len(route) for route in plan(frames).values()))
     vmem = pl.BlockSpec(memory_space=pltpu.VMEM)
+    anywhere = pl.BlockSpec(memory_space=pl.ANY)
     dma = pltpu.SemaphoreType.DMA
     refined = pl.pallas_call(
         functools.partial(kernel, frames, bands),
         out_shape=jax.ShapeDtypeStruct(band.shape, jnp.bfloat16),
-        in_specs=[vmem, vmem, pl.BlockSpec(memory_space=pltpu.SMEM), vmem, vmem],
+        in_specs=[anywhere, vmem, pl.BlockSpec(memory_space=pltpu.SMEM), anywhere, anywhere],
         out_specs=vmem,
         scratch_shapes=[
             pltpu.VMEM((LEVELS, local + 2 * HALO, channels, columns), jnp.bfloat16),
@@ -322,8 +347,11 @@
             pltpu.VMEM((8 + 2 * SPAN + 1, channels, columns), jnp.float32),
             pltpu.VMEM((local + 2 * REACH, 3 * channels, columns), jnp.bfloat16),
             pltpu.VMEM((local + 2, channels, columns), jnp.bfloat16),
-            pltpu.VMEM((3 * channels, 9 * channels), jnp.bfloat16),
-            pltpu.VMEM((3 * channels, 3 * channels), jnp.bfloat16),
+            pltpu.VMEM((6 * channels, 12 * channels), jnp.bfloat16),
+            pltpu.VMEM((6 * channels, 4 * channels), jnp.bfloat16),
+            pltpu.VMEM(uniting_weight.shape, jnp.bfloat16),
+            pltpu.VMEM(mixing_weight.shape, jnp.bfloat16),
+            dma((3,)),
             dma((LEVELS, 2)),
             dma((LEVELS, 2)),
             dma((total_refs, 4)),

time: 103 us -> 88.3 us (0.86); the launches traced: 103 us -> 87.3 us
  Pallas kernels: 98 us -> 82.1 us
    pallas_call x1, Pallas kernels: 98 us -> 82.1 us  [shards(): pl.pallas_call(functools.partial(kernel, frames, bands), out_shape=jax.Sh...]
where the time goes in v2:
time: 88.3 us; the launch traced here: 87.3 us
  Pallas kernels  82.1 us (93%)
  local copies, waits for them, and re-layouts  4.45 us (5%)
    pallas_call x1, Pallas kernels, shards(): pl.pallas_call(functools.partial(kernel, frames, bands), out_shape=jax.Sh...  82.1 us
    unnamed x10, local copies, waits for them, and re-layouts  4.45 us

profile of v2, /device:TPU:4, one launch (start us, length us, event | category | flops | bytes accessed | tf_op | source)
XLA Modules:
  0.0 87.3 jit_solution(5762982802794214869)
XLA Ops:
  0.0 0.0 copy-start.3
  0.0 0.7 copy-done.3
  0.7 0.1 copy.7.mask
  0.7 0.7 add_convert_fusion.grid_values
  1.5 0.0 copy-start
  1.5 1.0 %copy-done = bf16[1,16,64,256]{3,2,1,0:T(8,128)(2,1)S(1)} copy-done((bf16[1,16,64,256]{3,2,1,0:T(8,128)(2,1)S(1)}, bf16[1,16,64,256]{3,2,1,0:T(8,128)(2,1)}, u32[]{:S(2)}) %copy-start) | copy-done | bytes 524312
  2.5 0.0 copy-start.1
  2.5 1.0 %copy-done.1 = bf16[3,3,64,192]{3,2,1,0:T(8,128)(2,1)S(1)} copy-done((bf16[3,3,64,192]{3,2,1,0:T(8,128)(2,1)S(1)}, bf16[3,3,64,192]{3,2,1,0:T(8,128)(2,1)}, u32[]{:S(2)}) %copy-start.1) | copy-done | bytes 221208
  3.5 0.0 copy-start.2
  3.5 0.9 %copy-done.2 = bf16[3,3,64,64]{3,2,1,0:T(8,128)(2,1)S(1)} copy-done((bf16[3,3,64,64]{3,2,1,0:T(8,128)(2,1)S(1)}, bf16[3,3,64,64]{3,2,1,0:T(8,128)(2,1)}, u32[]{:S(2)}) %copy-start.2) | copy-done | bytes 73752
  4.4 82.1 %shard_map.64 = bf16[16,64,256]{2,1,0:T(8,128)(2,1)S(1)} custom-call(bf16[16,64,256]{2,1,0:T(8,128)(2,1)S(1)} %bitcast.5, f32[48,32]{1,0:T(8,128)S(1)} %add_convert_fusion.grid_values, s32[3,1]{1,0:T(4,128)S(1)} %copy.7.mask, bf16[3,3,64,192]{3,2,1,0:T(8,128)(2,1)S(1)} %copy-done.1, bf16[3,3,64,64]{3,2,1,0:T(8,128)(2,1)S(1)} %copy-done.2), custom_call_target="tpu_custom_call" | custom-call | tf_op jit(solution)/shard_map/pallas_call | solution.py:337
  86.5 0.8 copy.9
Async XLA Ops:
  0.0 0.7 copy-start.3
  1.5 1.0 %copy-start = (bf16[1,16,64,256]{3,2,1,0:T(8,128)(2,1)S(1)}, bf16[1,16,64,256]{3,2,1,0:T(8,128)(2,1)}, u32[]{:S(2)}) copy-start(bf16[1,16,64,256]{3,2,1,0:T(8,128)(2,1)} %param.6) | copy-start | bytes 1572868
  2.5 1.0 %copy-start.1 = (bf16[3,3,64,192]{3,2,1,0:T(8,128)(2,1)S(1)}, bf16[3,3,64,192]{3,2,1,0:T(8,128)(2,1)}, u32[]{:S(2)}) copy-start(bf16[3,3,64,192]{3,2,1,0:T(8,128)(2,1)} %uniting.1) | copy-start | bytes 663556
  3.5 0.9 %copy-start.2 = (bf16[3,3,64,64]{3,2,1,0:T(8,128)(2,1)S(1)}, bf16[3,3,64,64]{3,2,1,0:T(8,128)(2,1)}, u32[]{:S(2)}) copy-start(bf16[3,3,64,64]{3,2,1,0:T(8,128)(2,1)} %mixing.1) | copy-start | bytes 221188

commit v3 on v2

--- a/solution.py
+++ b/solution.py
@@ -10,6 +10,7 @@
 LEVELS = 3
 SPAN = 5
 HALO = 8
+PARTS = 4
 REACH = 2
 MESH = pl.DeviceIdType.MESH
 
@@ -37,7 +38,7 @@
     send_own, recv_own, send_ref, recv_ref, send_near, recv_near = scratch[12:]
     local = features.shape[0]
     channels, columns = features.shape[1:]
-    half = local // 2
+    size_of_part = local // PARTS
     first = {}
     for level in range(LEVELS - 1, -1, -1):
         first[level] = sum(len(routes[k]) for k in range(level + 1, LEVELS))
@@ -117,7 +118,7 @@
 
     def ref_copy(level, which, part):
         slot = first[level] + which
-        rows = pl.ds(HALO + part * half, half)
+        rows = pl.ds(HALO + part * size_of_part, size_of_part)
         return remote(
             own.at[level, rows],
             others.at[slot, rows],
@@ -126,14 +127,19 @@
             (lax.rem(t + routes[level][which], frames), r),
         )
 
-    def edge_copy(level, which, side):
+    def edge_side(part):
+        return 1 if part < PARTS // 2 else 0
+
+    def edge_copy(level, which, part):
         slot = first[level] + which
-        src, dst = (local, 0) if side == 0 else (HALO, HALO + local)
+        side = edge_side(part)
+        src = HALO + part * size_of_part
+        dst = src + local if side == 1 else src - local
         return remote(
-            others.at[slot, pl.ds(src, HALO)],
-            others.at[slot, pl.ds(dst, HALO)],
-            send_ref.at[slot, 2 + side],
-            recv_ref.at[slot, 2 + side],
+            others.at[slot, pl.ds(src, size_of_part)],
+            others.at[slot, pl.ds(dst, size_of_part)],
+            send_ref.at[slot, PARTS + part],
+            recv_ref.at[slot, PARTS + part],
             down if side == 0 else up,
         )
 
@@ -161,11 +167,14 @@
     def send_part(level, part):
         for which in range(len(routes[level])):
             ref_copy(level, which, part).start()
-        start(own_copy(level, 1 - part), 1 - part)
+        if part == (0 if routes[level] else PARTS // 2 - 1):
+            start(own_copy(level, 1), 1)
+        if part == PARTS - 1:
+            start(own_copy(level, 0), 0)
 
     band_copy.wait()
-    send_part(LEVELS - 1, 0)
-    send_part(LEVELS - 1, 1)
+    for part in range(PARTS):
+        send_part(LEVELS - 1, part)
     for side in (0, 1):
         start(near_copy(side), side)
 
@@ -285,42 +294,44 @@
         for side in (1, 0):
             received(own_copy(level, side), side)
         joined[:, 2 * channels : 3 * channels, :] = own[level, pl.ds(HALO - REACH, local + 2 * REACH)]
-        for part in (0, 1):
+        for part in range(PARTS):
             for which in range(count):
                 ref_copy(level, which, part).wait_recv()
-                start(edge_copy(level, which, 1 - part), 1 - part)
+                start(edge_copy(level, which, part), edge_side(part))
         for which in range(2):
             if which < count:
-                for side in (1, 0):
-                    received(edge_copy(level, which, side), side)
+                for part in range(PARTS):
+                    received(edge_copy(level, which, part), edge_side(part))
             source = others.at[first[level] + min(which, count - 1)] if count else own.at[level]
             warp(level, 2 * which, source, which * channels)
-        unite(0, half + 2)
-
-        @pl.when(jnp.logical_not(has_above))
-        def _():
-            activation[0] = jnp.zeros((channels, columns), jnp.bfloat16)
-
-        mix(level, 0, half)
-        if level > 0:
-            send_part(level - 1, 0)
-        unite(half + 2, local + 2)
-
-        @pl.when(jnp.logical_not(has_below))
-        def _():
-            activation[local + 1] = jnp.zeros((channels, columns), jnp.bfloat16)
-
-        mix(level, half, local)
-        if level > 0:
-            send_part(level - 1, 1)
+        for part in range(PARTS):
+            begin, end = part * size_of_part, (part + 1) * size_of_part
+            unite(begin + 2 if part else 0, end + 2)
+            if part == 0:
+
+                @pl.when(jnp.logical_not(has_above))
+                def _():
+                    activation[0] = jnp.zeros((channels, columns), jnp.bfloat16)
+
+            if part == PARTS - 1:
+
+                @pl.when(jnp.logical_not(has_below))
+                def _():
+                    activation[local + 1] = jnp.zeros((channels, columns), jnp.bfloat16)
+
+            mix(level, begin, end)
+            if level > 0:
+                send_part(level - 1, part)
 
     for side in (0, 1):
         sent(near_copy(side), side)
         for level in range(LEVELS):
             sent(own_copy(level, side), side)
-            for which in range(len(routes[level])):
-                ref_copy(level, which, side).wait_send()
-                sent(edge_copy(level, which, side), side)
+    for level in range(LEVELS):
+        for which in range(len(routes[level])):
+            for part in range(PARTS):
+                ref_copy(level, which, part).wait_send()
+                sent(edge_copy(level, which, part), edge_side(part))
 
 
 def shards(frames, bands, features, block_shift, quarter_pel, update_mask, uniting_weight, mixing_weight):
@@ -354,8 +365,8 @@
             dma((3,)),
             dma((LEVELS, 2)),
             dma((LEVELS, 2)),
-            dma((total_refs, 4)),
-            dma((total_refs, 4)),
+            dma((total_refs, 2 * PARTS)),
+            dma((total_refs, 2 * PARTS)),
             dma((2,)),
             dma((2,)),
         ],

time: 88.3 us -> 89.3 us (1.011)
  no operation moved by 1% of the time
where the time goes in v3:
time: 89.3 us; the launch traced here: 88.1 us
  Pallas kernels  82.9 us (93%)
  local copies, waits for them, and re-layouts  4.45 us (5%)
    pallas_call x1, Pallas kernels, shards(): pl.pallas_call(functools.partial(kernel, frames, bands), out_shape=jax.Sh...  82.9 us
    unnamed x10, local copies, waits for them, and re-layouts  4.45 us

profile of v3, /device:TPU:4, one launch (start us, length us, event | category | flops | bytes accessed | tf_op | source)
XLA Modules:
  0.0 88.1 jit_solution(1266510822564933642)
XLA Ops:
  0.0 0.0 copy-start.3
  0.0 0.7 copy-done.3
  0.7 0.1 copy.7.mask
  0.7 0.7 add_convert_fusion.grid_values
  1.5 0.0 copy-start
  1.5 1.0 %copy-done = bf16[1,16,64,256]{3,2,1,0:T(8,128)(2,1)S(1)} copy-done((bf16[1,16,64,256]{3,2,1,0:T(8,128)(2,1)S(1)}, bf16[1,16,64,256]{3,2,1,0:T(8,128)(2,1)}, u32[]{:S(2)}) %copy-start) | copy-done | bytes 524312
  2.5 0.0 copy-start.1
  2.5 1.0 %copy-done.1 = bf16[3,3,64,192]{3,2,1,0:T(8,128)(2,1)S(1)} copy-done((bf16[3,3,64,192]{3,2,1,0:T(8,128)(2,1)S(1)}, bf16[3,3,64,192]{3,2,1,0:T(8,128)(2,1)}, u32[]{:S(2)}) %copy-start.1) | copy-done | bytes 221208
  3.5 0.0 copy-start.2
  3.5 0.9 %copy-done.2 = bf16[3,3,64,64]{3,2,1,0:T(8,128)(2,1)S(1)} copy-done((bf16[3,3,64,64]{3,2,1,0:T(8,128)(2,1)S(1)}, bf16[3,3,64,64]{3,2,1,0:T(8,128)(2,1)}, u32[]{:S(2)}) %copy-start.2) | copy-done | bytes 73752
  4.4 82.9 %shard_map.64 = bf16[16,64,256]{2,1,0:T(8,128)(2,1)S(1)} custom-call(bf16[16,64,256]{2,1,0:T(8,128)(2,1)S(1)} %bitcast.5, f32[48,32]{1,0:T(8,128)S(1)} %add_convert_fusion.grid_values, s32[3,1]{1,0:T(4,128)S(1)} %copy.7.mask, bf16[3,3,64,192]{3,2,1,0:T(8,128)(2,1)S(1)} %copy-done.1, bf16[3,3,64,64]{3,2,1,0:T(8,128)(2,1)S(1)} %copy-done.2), custom_call_target="tpu_custom_call" | custom-call | tf_op jit(solution)/shard_map/pallas_call | solution.py:348
  87.3 0.8 copy.9
Async XLA Ops:
  0.0 0.7 copy-start.3
  1.5 1.0 %copy-start = (bf16[1,16,64,256]{3,2,1,0:T(8,128)(2,1)S(1)}, bf16[1,16,64,256]{3,2,1,0:T(8,128)(2,1)}, u32[]{:S(2)}) copy-start(bf16[1,16,64,256]{3,2,1,0:T(8,128)(2,1)} %param.6) | copy-start | bytes 1572868
  2.5 1.0 %copy-start.1 = (bf16[3,3,64,192]{3,2,1,0:T(8,128)(2,1)S(1)}, bf16[3,3,64,192]{3,2,1,0:T(8,128)(2,1)}, u32[]{:S(2)}) copy-start(bf16[3,3,64,192]{3,2,1,0:T(8,128)(2,1)} %uniting.1) | copy-start | bytes 663556
  3.5 0.9 %copy-start.2 = (bf16[3,3,64,64]{3,2,1,0:T(8,128)(2,1)S(1)}, bf16[3,3,64,64]{3,2,1,0:T(8,128)(2,1)}, u32[]{:S(2)}) copy-start(bf16[3,3,64,64]{3,2,1,0:T(8,128)(2,1)} %mixing.1) | copy-start | bytes 221188
